TPU v7x, 32 devices: a whole 2x2x4 slice. The times are simulated.
32 devices in a mesh: dp: 8 (over y, x, core), col: 4 (over z).
Axes of the slice: x: 2, y: 2, z: 4, core: 2. Of those that a mesh axis runs over, the one named last changes fastest.
Arguments:
- item_ids: int32 [256, 32], P('dp'), may hold values from 0 to 37482
- target_ids: int32 [256, 32], P('dp'), may hold values from 0 to 37482
- negative_ids: int32 [2048], replicated, may hold values from 0 to 37482
- reset_mask: int32 [256, 32], P('dp'), may hold values 0 or 1
- carry_flags: int32 [256], P('dp'), may hold values 0 or 1
- carried_state: float32 [256, 1000], P('dp', 'col'), may hold values from -3 to 3
- embed_table: float32 [1000, 37888], P('col'), may hold values from -6 to 6
- input_weight: float32 [3, 1000, 1000], P(None, 'col'), may hold values from -0.1875 to 0.1875
- hidden_weight: float32 [3, 1000, 1000], P(None, 'col'), may hold values from -0.1875 to 0.1875
- gate_bias: float32 [3, 1000], P(None, 'col'), may hold values from -3 to 3
- hidden_bias: float32 [1000], P('col'), may hold values from -3 to 3
- out_table: float32 [1000, 37888], P('col'), may hold values from -0.5 to 0.5
- out_bias: float32 [37888], replicated, may hold values from -3 to 3
Outputs:
- loss: float32 [256, 32], P('dp')
- grad_embed: float32 [1000, 37888], P('col', 'dp')
- grad_input_weight: float32 [3, 1000, 1000], P(None, 'col')
- grad_hidden_weight: float32 [3, 1000, 1000], P(None, 'col')
- grad_gate_bias: float32 [3, 1000], P(None, 'col')
- grad_hidden_bias: float32 [1000], P('col')
- grad_out_table: float32 [1000, 37888], P('col', 'dp')
- grad_out_bias: float32 [37888], P('dp')
- grad_carried: float32 [256, 1000], P('dp', 'col')
All inputs are finite; a program needn't handle non-finite values. No bound on the sum of `reset_mask` or of `carry_flags` on one device may be relied on, other than what follows from the above.
Results may differ from a plain program's by a relative error of at most 0.0003.
Values sent between devices are 32-bit elements; how exact they have to be, the bound alone decides.
A program may use at most 384 MiB of HBM per device.

v0:
```python
import functools

import jax
import jax.numpy as jnp
from jax import lax
from jax.experimental import pallas as pl
from jax.experimental.pallas import tpu as pltpu
from jax.sharding import PartitionSpec as P

LANES = 128
ROWS8 = 8
VMEM_BYTES = 60 << 20
f32 = jnp.float32
bf16 = jnp.bfloat16
high = lax.Precision.HIGH
MESH = pl.DeviceIdType.MESH


def round_up(value, unit):
    return -(-value // unit) * unit


def params():
    return pltpu.CompilerParams(vmem_limit_bytes=VMEM_BYTES)


def takes(micros):
    return pl.CostEstimate(flops=int(micros * 1.1e9), bytes_accessed=1 << 20, transcendentals=0)


def in_vmem():
    return pl.BlockSpec(memory_space=pltpu.VMEM)


def in_smem():
    return pl.BlockSpec(memory_space=pltpu.SMEM)


def gather_kernel(chunk, count, width, ids, table, bias, out, padded, turned):
    step = pl.program_id(0)

    @pl.when(step == 0)
    def _():
        padded[...] = jnp.zeros_like(padded)

    padded[0:width, :] = table[...]
    padded[width : width + 1, :] = bias[...]
    turned[pl.ds(pl.multiple_of(step * chunk, chunk), chunk), :] = padded[...].T

    @pl.when(step == pl.num_programs(0) - 1)
    def _():
        def body(block, carry):
            for j in range(ROWS8):
                row = ids[block * ROWS8 + j]
                out[pl.ds(block * ROWS8 + j, 1), :] = turned[pl.ds(row, 1), :]
            return carry

        lax.fori_loop(0, count // ROWS8, body, 0)


def gather_rows(table, bias, ids, block):
    width, rows = table.shape
    count = ids.shape[0]
    chunk = LANES * max(k for k in range(1, 9) if rows % (LANES * k) == 0)
    return pl.pallas_call(
        functools.partial(gather_kernel, chunk, count, width),
        out_shape=jax.ShapeDtypeStruct((count, block), f32),
        grid_spec=pltpu.PrefetchScalarGridSpec(
            num_scalar_prefetch=1,
            grid=(rows // chunk,),
            in_specs=[
                pl.BlockSpec((width, chunk), lambda i, ids: (0, i)),
                pl.BlockSpec((1, chunk), lambda i, ids: (0, i)),
            ],
            out_specs=pl.BlockSpec((count, block), lambda i, ids: (0, 0)),
            scratch_shapes=[pltpu.VMEM((block, chunk), f32), pltpu.VMEM((rows, block), f32)],
        ),
        compiler_params=params(),
    )(ids, table, bias)


def scatter_kernel(width, n_lists, *refs):
    bounds = refs[0]
    lists = refs[1 : 1 + 3 * n_lists]
    out, bias_out, acc = refs[1 + 3 * n_lists :]
    acc[...] = jnp.zeros_like(acc)
    low = bounds[0]
    for k in range(n_lists):
        rows_of, ids, data = lists[3 * k : 3 * k + 3]

        def body(i, carry):
            spot = pl.ds(ids[i] - low, 1)
            acc[spot, :] = acc[spot, :] + data[pl.ds(rows_of[i], 1), :]
            return carry

        lax.fori_loop(bounds[1 + 2 * k], bounds[2 + 2 * k], body, 0)
    for j in range(acc.shape[0] // LANES):
        cols = slice(j * LANES, (j + 1) * LANES)
        turned = acc[cols, :].T
        out[:, cols] = turned[:width]
        bias_out[:, cols] = turned[width : width + 1]


def scatter_rows(lists, low, own_rows, width, block):
    ends = [low]
    operands, specs = [], []
    for order, ids, data in lists:
        ends += [jnp.sum(ids < low, dtype=jnp.int32), jnp.sum(ids < low + own_rows, dtype=jnp.int32)]
        operands += [order, ids, data]
        specs += [in_smem(), in_smem(), in_vmem()]
    return pl.pallas_call(
        functools.partial(scatter_kernel, width, len(lists)),
        out_shape=(
            jax.ShapeDtypeStruct((width, own_rows), f32),
            jax.ShapeDtypeStruct((1, own_rows), f32),
        ),
        in_specs=[in_smem()] + specs,
        out_specs=(in_vmem(), in_vmem()),
        scratch_shapes=[pltpu.VMEM((own_rows, block), f32)],
        cost_estimate=takes(20),
        compiler_params=params(),
    )(jnp.stack(ends), *operands)


def split_weight(weight, high_part, low_part):
    step = 128

    @pl.loop(0, weight.shape[0] // step)
    def _(i):
        rows = pl.ds(pl.multiple_of(i * step, step), step)
        value = weight[rows, :]
        top = value.astype(bf16)
        high_part[rows, :] = top
        low_part[rows, :] = (value - top.astype(f32)).astype(bf16)


def two_part(value):
    top = value.astype(bf16).astype(f32)
    return jnp.concatenate([top, value - top], axis=0).astype(bf16)


def forward_kernel(
    steps,
    width,
    hidden,
    entering,
    inputs,
    keep,
    start,
    prevs,
    resets,
    updates,
    cands,
    inners,
    outs,
    w_high,
    w_low,
    x_gates,
    hid_buf,
    in_buf,
    pair_buf,
    sem,
    travel=None,
):
    rows_per, units = start.shape
    step_rows = hid_buf.shape[1]
    chunks = hidden.shape[0] // step_rows

    def load(i, slot):
        rows = pl.ds(pl.multiple_of(i * step_rows, step_rows), step_rows)
        return (
            pltpu.make_async_copy(hidden.at[rows], hid_buf.at[slot], sem.at[0, slot]),
            pltpu.make_async_copy(entering.at[rows], in_buf.at[slot], sem.at[1, slot]),
        )

    for copy in load(0, 0):
        copy.start()
    timeline = travel() if travel else ()
    top = inputs[...].astype(bf16)
    pair_buf[0] = top
    pair_buf[1] = (inputs[...] - top.astype(f32)).astype(bf16)

    @pl.loop(0, chunks)
    def _(i):
        slot = lax.rem(i, 2)

        @pl.when(i + 1 < chunks)
        def _():
            for copy in load(i + 1, 1 - slot):
                copy.start()

        for copy in load(i, slot):
            copy.wait()
        cols = pl.ds(pl.multiple_of(i * step_rows, step_rows), step_rows)
        turned = hid_buf[slot].T
        first = turned.astype(bf16)
        w_high[:, cols] = first
        w_low[:, cols] = (turned - first.astype(f32)).astype(bf16)
        value = in_buf[slot]
        first = value.astype(bf16)
        second = (value - first.astype(f32)).astype(bf16)
        over = (((1,), (1,)), ((), ()))
        x_gates[:, cols] = (
            lax.dot_general(pair_buf[0], first, over, preferred_element_type=f32)
            + lax.dot_general(pair_buf[1], first, over, preferred_element_type=f32)
            + lax.dot_general(pair_buf[0], second, over, preferred_element_type=f32)
        )

    lane = lax.broadcasted_iota(jnp.int32, (rows_per, units), 1)

    def step(t, state):
        rows = pl.ds(pl.multiple_of(t * rows_per, rows_per), rows_per)
        prev = jnp.where(lane == width, 1.0, keep[rows, :] * state)
        pair = two_part(prev)

        def gate(g):
            cols = slice(g * units, (g + 1) * units)
            first = jnp.dot(pair, w_high[:, cols], preferred_element_type=f32)
            second = jnp.dot(pair, w_low[:, cols], preferred_element_type=f32)
            return first[:rows_per] + first[rows_per:] + second[:rows_per], cols

        h_reset, cols = gate(0)
        reset = jax.nn.sigmoid(x_gates[rows, cols] + h_reset)
        h_update, cols = gate(1)
        update = jax.nn.sigmoid(x_gates[rows, cols] + h_update)
        inner, cols = gate(2)
        cand = jnp.tanh(x_gates[rows, cols] + reset * inner)
        new = (1.0 - update) * cand + update * prev
        prevs[rows, :] = prev
        resets[rows, :] = reset
        updates[rows, :] = update
        cands[rows, :] = cand
        inners[rows, :] = inner
        outs[rows, :] = new
        return new

    state, done = start[...], 0
    for share_done, actions in timeline:
        until = int(share_done * steps)
        if until > done:
            state, done = lax.fori_loop(done, until, step, state), until
        for action, argument in actions:
            action(argument)
    lax.fori_loop(done, steps, step, state)


def forward_travel_kernel(steps, width, hidden, entering, inputs, keep, start, neg_own, target_own, *refs):
    saved, (neg_all, targets), scratch = refs[:6], refs[6:8], refs[8:]
    z_rows, target_send, target_recv, target_local, row_local, row_send, row_recv = scratch[7:]
    spot = Spot()
    rows = RowsFlow(spot, neg_own, z_rows, neg_all, row_local, row_send, row_recv, same=True)
    copies = []

    def begin_targets(_):
        keep_own = pltpu.make_async_copy(target_own.at[spot.c], targets.at[spot.c], target_local.at[0])
        keep_own.start()
        copies.append(keep_own)
        for m, z in enumerate(spot.z_to):
            copies.append(
                remote(target_own.at[z], targets.at[spot.c], target_send.at[m], target_recv.at[m], (spot.d, z))
            )

    def travel():
        spot.greet_all()
        rows.begin()
        return (
            (0.0, ((rows.forward, 0),)),
            (0.1, ((rows.spread, 1),)),
            (0.2, ((rows.far, 0),)),
            (0.3, ((rows.forward, 1), (rows.spread, 2), (begin_targets, None))),
            (0.4, ((rows.far, 1),)),
            (0.5, ((rows.forward, 2), (rows.spread, 3))),
            (0.6, ((rows.far, 2),)),
            (0.7, ((rows.forward, 3),)),
            (0.85, ((rows.far, 3),)),
        )

    forward_kernel(steps, width, hidden, entering, inputs, keep, start, *saved, *scratch[:7], travel=travel)
    rows.close()
    for copy in copies:
        copy.wait()


def forward_scratch(hidden, inputs):
    events, units = inputs.shape
    step_rows = units // 4
    return [
        pltpu.VMEM(hidden.shape[::-1], bf16),
        pltpu.VMEM(hidden.shape[::-1], bf16),
        pltpu.VMEM((events, hidden.shape[0]), f32),
        pltpu.VMEM((2, step_rows, units), f32),
        pltpu.VMEM((2, step_rows, units), f32),
        pltpu.VMEM((2, events, units), bf16),
        pltpu.SemaphoreType.DMA((2, 2)),
    ]


def run_forward(hidden, entering, inputs, keep, start, steps, width):
    saved = jax.ShapeDtypeStruct(inputs.shape, f32)
    hbm = pl.BlockSpec(memory_space=pl.ANY)
    return pl.pallas_call(
        functools.partial(forward_kernel, steps, width),
        out_shape=(saved,) * 6,
        in_specs=[hbm, hbm] + [in_vmem()] * 3,
        out_specs=(in_vmem(),) * 6,
        scratch_shapes=forward_scratch(hidden, inputs),
        cost_estimate=takes(75),
        compiler_params=params(),
    )(hidden, entering, inputs, keep, start)


def run_forward_travel(hidden, entering, inputs, keep, start, neg_own, target_own, steps, width, collective_id):
    saved = jax.ShapeDtypeStruct(inputs.shape, f32)
    hbm = pl.BlockSpec(memory_space=pl.ANY)
    dma = pltpu.SemaphoreType.DMA
    return pl.pallas_call(
        functools.partial(forward_travel_kernel, steps, width),
        out_shape=(saved,) * 6
        + (jax.ShapeDtypeStruct((8, 4) + neg_own.shape, f32), jax.ShapeDtypeStruct(target_own.shape, f32)),
        in_specs=[hbm, hbm] + [in_vmem()] * 3 + [hbm, hbm],
        out_specs=(in_vmem(),) * 6 + (hbm, hbm),
        scratch_shapes=forward_scratch(hidden, inputs)
        + [pltpu.VMEM((4,) + neg_own.shape, f32), dma((3,)), dma((3,)), dma((1,)), dma((4,)), dma((4, 9)), dma((4, 9))],
        cost_estimate=takes(75),
        compiler_params=pltpu.CompilerParams(
            collective_id=collective_id, has_side_effects=True, vmem_limit_bytes=VMEM_BYTES
        ),
    )(hidden, entering, inputs, keep, start, neg_own, target_own)


def backward_kernel(
    steps, weight, douts, keep, prevs, resets, updates, cands, inners, dgates, dstart, w_high, w_low
):
    rows_per, units = dstart.shape
    split_weight(weight, w_high, w_low)

    def step(i, dstate):
        t = steps - 1 - i
        rows = pl.ds(pl.multiple_of(t * rows_per, rows_per), rows_per)
        reset, update, cand = resets[rows, :], updates[rows, :], cands[rows, :]
        dh = douts[rows, :] + dstate
        dcand = dh * (1.0 - update) * (1.0 - cand * cand)
        dreset = dcand * inners[rows, :] * reset * (1.0 - reset)
        dupdate = dh * (prevs[rows, :] - cand) * update * (1.0 - update)
        dinner = dcand * reset
        dgates[rows, 0:units] = dreset
        dgates[rows, units : 2 * units] = dupdate
        dgates[rows, 2 * units : 3 * units] = dinner
        dgates[rows, 3 * units : 4 * units] = dcand
        total = dh * update
        for g, part in enumerate((dreset, dupdate, dinner)):
            pair = two_part(part)
            sect = slice(g * units, (g + 1) * units)
            first = jnp.dot(pair, w_high[sect, :], preferred_element_type=f32)
            second = jnp.dot(pair, w_low[sect, :], preferred_element_type=f32)
            total = total + (first[:rows_per] + first[rows_per:] + second[:rows_per])
        return keep[rows, :] * total

    dstart[...] = lax.fori_loop(0, steps, step, jnp.zeros((rows_per, units), f32))


def run_backward(weight, douts, keep, saved, rows_per, steps):
    events, units = douts.shape
    return pl.pallas_call(
        functools.partial(backward_kernel, steps),
        out_shape=(
            jax.ShapeDtypeStruct((events, 4 * units), f32),
            jax.ShapeDtypeStruct((rows_per, units), f32),
        ),
        in_specs=[in_vmem()] * 8,
        out_specs=(in_vmem(),) * 2,
        scratch_shapes=[pltpu.VMEM(weight.shape, bf16)] * 2,
        cost_estimate=takes(67),
        compiler_params=params(),
    )(weight, douts, keep, *saved)


def place():
    d = lax.axis_index("dp")
    c = lax.axis_index("col")
    return d // 4, (d // 2) % 2, d % 2, c, d


def greet(partners):
    barrier = pltpu.get_barrier_semaphore()
    for partner in partners:
        pl.semaphore_signal(barrier, inc=1, device_id=partner, device_id_type=MESH)
    pl.semaphore_wait(barrier, len(partners))


class Spot:
    def __init__(self):
        self.y, self.x, self.k, self.c, self.d = place()
        y, x, k, c, d = self.y, self.x, self.k, self.c, self.d
        self.x_d, self.y_d, self.core_d = d + 2 - 4 * x, d + 4 - 8 * y, d + 1 - 2 * k
        self.far_d = d + 6 - 4 * x - 8 * y
        self.core_to, self.x_to, self.y_to, self.far_to = (self.core_d, c), (self.x_d, c), (self.y_d, c), (self.far_d, c)
        self.z_to = (c + 1 - 2 * lax.rem(c, 2), lax.rem(c + 2, 4), 3 - c)

    def greet_all(self):
        greet([self.core_to, self.x_to, self.y_to, self.far_to] + [(self.d, z) for z in self.z_to])


def remote(source, target, send, recv, to):
    copy = pltpu.make_async_remote_copy(
        src_ref=source, dst_ref=target, send_sem=send, recv_sem=recv, device_id=to, device_id_type=MESH
    )
    copy.start()
    return copy


class RowsFlow:
    def __init__(self, spot, outgoing, z_rows, every, local_sem, send_sem, recv_sem, same=False):
        self.spot, self.outgoing, self.z_rows, self.every = spot, outgoing, z_rows, every
        self.local_sem, self.send_sem, self.recv_sem = local_sem, send_sem, recv_sem
        self.started = {}
        self.rows = every.shape[2]
        self.sources = (spot.c,) + spot.z_to
        self.same = same

    def send(self, u, slot, source, target, to):
        return remote(source, target, self.send_sem.at[u, slot], self.recv_sem.at[u, slot], to)

    def begin(self):
        spot = self.spot
        for m in range(3):
            z = spot.z_to[m]
            source = self.outgoing if self.same else self.outgoing.at[z]
            self.started["z", m] = self.send(1 + m, 0, source, self.z_rows.at[spot.c], (spot.d, z))
        self.spread(0)

    def spread(self, u):
        spot, src = self.spot, self.sources[u]
        if u > 0:
            self.started["z", u - 1].wait_recv()
            source = self.z_rows.at[src, 0 : self.rows]
        else:
            source = self.outgoing if self.same else self.outgoing.at[src, 0 : self.rows]
        target = self.every.at[spot.d, src]
        keep = pltpu.make_async_copy(source, target, self.local_sem.at[u])
        keep.start()
        self.started["keep", u] = keep
        for slot, (name, to) in enumerate((("x", spot.x_to), ("y", spot.y_to), ("c", spot.core_to))):
            self.started[name, u] = self.send(u, 1 + slot, source, target, to)

    def forward(self, u):
        spot, src, mid = self.spot, self.sources[u], self.rows // 2
        self.started["x", u].wait_recv()
        piece = self.every.at[spot.x_d, src, 0:mid]
        self.started["xy", u] = self.send(u, 4, piece, piece, spot.y_to)
        piece = self.every.at[spot.x_d, src]
        self.started["xc", u] = self.send(u, 5, piece, piece, spot.core_to)
        self.started["y", u].wait_recv()
        piece = self.every.at[spot.y_d, src, mid : self.rows]
        self.started["yx", u] = self.send(u, 6, piece, piece, spot.x_to)
        piece = self.every.at[spot.y_d, src]
        self.started["yc", u] = self.send(u, 7, piece, piece, spot.core_to)

    def far(self, u):
        spot, src = self.spot, self.sources[u]
        self.started["xy", u].wait_recv()
        self.started["yx", u].wait_recv()
        piece = self.every.at[spot.far_d, src]
        self.started["fc", u] = self.send(u, 8, piece, piece, spot.core_to)

    def close(self):
        for u in range(4):
            for name in ("c", "xc", "yc", "fc"):
                self.started[name, u].wait_recv()
            self.started["keep", u].wait()
        for (name, _), copy in self.started.items():
            if name != "keep":
                copy.wait_send()


class SumFlow:
    def __init__(self, spot, mine, core_in, x_in, y_in, xy_in, yx_in, z_in, total, out_at, local_sem, send_sem, recv_sem):
        self.spot, self.mine, self.core_in, self.out_at = spot, mine, core_in, out_at
        self.x_in, self.y_in, self.xy_in, self.yx_in, self.z_in, self.total = x_in, y_in, xy_in, yx_in, z_in, total
        self.local_sem, self.send_sem, self.recv_sem = local_sem, send_sem, recv_sem
        self.started = [{} for _ in range(mine.shape[0])]
        self.half = mine.shape[4] // 2

    def send(self, j, slot, source, target, to):
        return remote(source, target, self.send_sem.at[j, slot], self.recv_sem.at[j, slot], to)

    def over_core(self, j, source):
        self.started[j]["core"] = self.send(j, 0, source, self.core_in.at[j], self.spot.core_to)

    def core(self, j):
        spot, mine, half, started = self.spot, self.mine, self.half, self.started[j]
        started["core"].wait_recv()

        @pl.loop(0, 4)
        def _(a):
            for b in range(2):
                for e in range(2):
                    mine[j, a, b, e] = mine[j, a, b, e] + self.core_in[j, a, b, e]

        started["x"] = self.send(j, 1, mine.at[j, :, :, 1 - spot.x, 0:half], self.x_in.at[j], spot.x_to)
        started["y"] = self.send(j, 2, mine.at[j, :, 1 - spot.y, :, half : 2 * half], self.y_in.at[j], spot.y_to)

    def first(self, j):
        spot, mine, half, started = self.spot, self.mine, self.half, self.started[j]
        x, y = spot.x, spot.y
        started["x"].wait_recv()
        for a in range(4):
            for b in range(2):
                mine[j, a, b, x, 0:half] = mine[j, a, b, x, 0:half] + self.x_in[j, a, b]
        started["xy"] = self.send(j, 3, mine.at[j, :, 1 - y, x, 0:half], self.xy_in.at[j], spot.y_to)
        started["y"].wait_recv()
        for a in range(4):
            for e in range(2):
                mine[j, a, y, e, half : 2 * half] = mine[j, a, y, e, half : 2 * half] + self.y_in[j, a, e]
        started["yx"] = self.send(j, 4, mine.at[j, :, y, 1 - x, half : 2 * half], self.yx_in.at[j], spot.x_to)

    def second(self, j):
        spot, mine, half, started = self.spot, self.mine, self.half, self.started[j]
        x, y = spot.x, spot.y
        started["xy"].wait_recv()
        started["yx"].wait_recv()
        for a in range(4):
            mine[j, a, y, x, 0:half] = mine[j, a, y, x, 0:half] + self.xy_in[j, a]
            mine[j, a, y, x, half : 2 * half] = mine[j, a, y, x, half : 2 * half] + self.yx_in[j, a]
        for m in range(3):
            z = spot.z_to[m]
            started["z", m] = self.send(j, 5 + m, mine.at[j, z, y, x], self.z_in.at[j, m], (spot.d, z))

    def along(self, j):
        spot, started, total = self.spot, self.started[j], self.total
        for m in range(3):
            started["z", m].wait_recv()
        own = self.mine[j, spot.c, spot.y, spot.x]
        total[j] = ((own + self.z_in[j, 0]) + self.z_in[j, 1]) + self.z_in[j, 2]
        target = self.out_at(j, spot.d)
        started["keep"] = pltpu.make_async_copy(total.at[j], target, self.local_sem.at[j])
        started["keep"].start()
        pairs = (("gx", spot.x_to), ("gy", spot.y_to), ("gf", spot.far_to), ("gc", spot.core_to))
        for slot, (name, to) in enumerate(pairs):
            started[name] = self.send(j, 8 + slot, total.at[j], target, to)

    def share(self, j):
        spot, started = self.spot, self.started[j]
        for slot, (name, to) in enumerate((("gx", spot.x_to), ("gy", spot.y_to), ("gf", spot.far_to))):
            started[name].wait_recv()
            piece = self.out_at(j, to[0])
            started["c" + name] = self.send(j, 12 + slot, piece, piece, spot.core_to)

    def end(self, j, core_sent=False):
        started = self.started[j]
        for name in ("gc", "cgx", "cgy", "cgf"):
            started[name].wait_recv()
        for name, copy in started.items():
            if name == "keep":
                copy.wait()
            elif not (name == "core" and core_sent):
                copy.wait_send()


def sum_scratch(jobs, piece, lanes):
    half = piece // 2
    return [
        pltpu.VMEM((jobs, 4, 2, 2, piece, lanes), f32),
        pltpu.VMEM((jobs, 4, 2, 2, piece, lanes), f32),
        pltpu.VMEM((jobs, 4, 2, half, lanes), f32),
        pltpu.VMEM((jobs, 4, 2, half, lanes), f32),
        pltpu.VMEM((jobs, 4, half, lanes), f32),
        pltpu.VMEM((jobs, 4, half, lanes), f32),
        pltpu.VMEM((jobs, 3, piece, lanes), f32),
        pltpu.VMEM((jobs, piece, lanes), f32),
    ]


def flow_sems(jobs):
    dma = pltpu.SemaphoreType.DMA
    return [dma((jobs,)), dma((jobs, 15)), dma((jobs, 15)), dma((4,)), dma((4, 9)), dma((4, 9))]


GATE_OF = ((0, 1, 3), (0, 1, 2))


def split_two(value):
    top = value.astype(bf16)
    return top, (value - top.astype(f32)).astype(bf16)


def three_products(first, second, over):
    def product(a, b):
        return lax.dot_general(a, b, (over, ((), ())), preferred_element_type=f32)

    return product(first[0], second[0]) + product(first[1], second[0]) + product(first[0], second[1])


def tail_kernel(
    inputs,
    prevs,
    dgates,
    dstart,
    entering,
    out,
    item_all,
    start_all,
    mine,
    core_in,
    x_in,
    y_in,
    xy_in,
    yx_in,
    z_in,
    total,
    core_out,
    turned,
    acts,
    flow,
    w_flow,
    din,
    z_rows,
    flow_sem,
    start_sem,
    sum_local,
    sum_send,
    sum_recv,
    row_local,
    row_send,
    row_recv,
):
    spot = Spot()
    spot.greet_all()
    c, k = spot.c, spot.k
    jobs, _, _, _, piece, units = mine.shape
    block = din.shape[2]
    events = acts.shape[2]
    gates = jobs // 2
    sums = SumFlow(
        spot, mine, core_in, x_in, y_in, xy_in, yx_in, z_in, total,
        lambda j, d: out.at[j // gates, j % gates, d], sum_local, sum_send, sum_recv,
    )
    rows = RowsFlow(spot, din, z_rows, item_all, row_local, row_send, row_recv)

    def gate_cols(g):
        return dgates.at[:, pl.ds(g * units, units)]

    queue = [inputs, gate_cols(0), gate_cols(1), gate_cols(3), prevs, gate_cols(2)]

    def flow_copy(n):
        return pltpu.make_async_copy(queue[n], flow.at[n % 2], flow_sem.at[n % 2])

    def w_copy(n, slot):
        rows = pl.ds(pl.multiple_of(n * block, block), block)
        return pltpu.make_async_copy(entering.at[rows], w_flow.at[slot], flow_sem.at[2 + slot])

    flow_copy(0).start()
    flow_copy(1).start()
    w_copy(0, 0).start()

    def next_flow(n):
        if n + 2 < len(queue):
            flow_copy(n + 2).start()

    def take_act(n, w):
        flow_copy(n).wait()
        acts[w, 0], acts[w, 1] = split_two(flow[n % 2])
        next_flow(n)

    def take_gate(n, g, at):
        flow_copy(n).wait()

        @pl.loop(0, 4)
        def _(b):
            cols = pl.ds(pl.multiple_of(b * block, block), block)
            value = flow[n % 2, :, cols]
            turned[g, 0, b], turned[g, 1, b] = split_two(value.T)
            if at is not None:
                chunk = 4 * at + b
                slot = lax.rem(b, 2)

                @pl.when(chunk + 1 < 12)
                def _():
                    w_copy(chunk + 1, 1 - slot).start()

                w_copy(chunk, slot).wait()
                share = three_products(split_two(value), split_two(w_flow[slot]), ((1,), (0,)))
                for e in range(4):
                    part = share[:, e * block : (e + 1) * block]
                    if at == 0:
                        before = jnp.where(b == 0, 0.0, din[e, 0:events, :])
                    else:
                        before = din[e, 0:events, :]
                    din[e, 0:events, :] = before + part

        next_flow(n)

    def rows_begin():
        for e in range(4):
            din[e, events:, :] = dstart[:, e * block : (e + 1) * block]
        rows.begin()

    def rows_end():
        keeps = [
            pltpu.make_async_copy(din.at[c, events:], start_all.at[c], start_sem.at[0]),
        ] + [
            pltpu.make_async_copy(z_rows.at[z, events:], start_all.at[z], start_sem.at[1 + m])
            for m, z in enumerate(spot.z_to)
        ]
        for keep in keeps:
            keep.start()
        rows.close()
        for keep in keeps:
            keep.wait()

    def partial(j):
        w, g = j // gates, GATE_OF[j // gates][j % gates]
        slot = j % 2
        if j >= 2:
            sums.started[j - 2]["core"].wait_send()

        @pl.loop(0, 4)
        def _(b):
            value = three_products(
                (turned[g, 0, b], turned[g, 1, b]), (acts[w, 0], acts[w, 1]), ((1,), (0,))
            ).reshape(2, 2, 2, piece, units)
            for p in range(2):
                for q in range(2):
                    mine[j, b, p, q] = jnp.where(k == 0, value[p, q, 0], value[p, q, 1])
                    core_out[slot, b, p, q] = jnp.where(k == 0, value[p, q, 1], value[p, q, 0])

        sums.over_core(j, core_out.at[slot])

    A, B, C, Z, S = sums.core, sums.first, sums.second, sums.along, sums.share

    def E(j):
        sums.end(j, core_sent=j < jobs - 2)

    take_act(0, 0)
    take_gate(1, 0, 0)
    partial(0)
    take_gate(2, 1, 1)
    partial(1)
    A(0)
    take_gate(3, 3, 2)
    rows_begin()
    partial(2)
    A(1)
    take_act(4, 1)
    partial(3)
    A(2), B(0), rows.spread(1), rows.forward(0)
    partial(4)
    A(3), B(1), C(0), rows.spread(2), rows.forward(1), rows.far(0)
    take_gate(5, 2, None)
    partial(5)
    A(4), B(2), C(1), Z(0), rows.spread(3), rows.forward(2), rows.far(1)
    A(5), B(3), C(2), Z(1), S(0), rows.forward(3), rows.far(2)
    B(4), C(3), Z(2), S(1), E(0), rows.far(3)
    B(5), C(4), Z(3), S(2), E(1)
    C(5), Z(4), S(3), E(2)
    rows_end()
    Z(5), S(4), E(3)
    S(5), E(4), E(5)


def run_tail(inputs, prevs, dgates, dstart, entering, collective_id):
    events, units = inputs.shape
    gates, block = 3, units // 4
    piece = block // 8
    jobs = 2 * gates
    start_rows = dstart.shape[0]
    hbm = pl.BlockSpec(memory_space=pl.ANY)
    grads, item_all, start_all = pl.pallas_call(
        tail_kernel,
        out_shape=(
            jax.ShapeDtypeStruct((2, gates, 8, piece, units), f32),
            jax.ShapeDtypeStruct((8, 4, events, block), f32),
            jax.ShapeDtypeStruct((4, start_rows, block), f32),
        ),
        in_specs=[hbm, hbm, hbm, pl.BlockSpec(memory_space=pltpu.VMEM), hbm],
        out_specs=(hbm, hbm, hbm),
        scratch_shapes=sum_scratch(jobs, piece, units)
        + [
            pltpu.VMEM((2, 4, 2, 2, piece, units), f32),
            pltpu.VMEM((4, 2, 4, block, events), bf16),
            pltpu.VMEM((2, 2, events, units), bf16),
            pltpu.VMEM((2, events, units), f32),
            pltpu.VMEM((2, block, units), f32),
            pltpu.VMEM((4, events + start_rows, block), f32),
            pltpu.VMEM((4, events + start_rows, block), f32),
            pltpu.SemaphoreType.DMA((4,)),
            pltpu.SemaphoreType.DMA((4,)),
        ]
        + flow_sems(jobs),
        cost_estimate=takes(190),
        compiler_params=pltpu.CompilerParams(
            collective_id=collective_id, has_side_effects=True, vmem_limit_bytes=VMEM_BYTES
        ),
    )(inputs, prevs, dgates, dstart, entering)
    return grads.reshape(2, gates, 8 * piece, units), item_all, start_all


UNITS = ((0, 0), (0, 1), (1, 0), (0, 2), (1, 1), (1, 2))


def head_kernel(
    chunk,
    width,
    item_ids,
    out_ids,
    embed,
    table,
    bias,
    own_in,
    own_hid,
    carried,
    own_ids,
    all_in,
    all_hid,
    arrived,
    all_ids,
    out_rows,
    padded,
    turned,
    item_rows,
    held,
    local_sem,
    send_sem,
    recv_sem,
    row_send,
    row_recv,
    id_send,
    id_recv,
):
    y, x, k, c, d = place()
    i = pl.program_id(0)
    n = pl.num_programs(0) // 2
    core_to, x_to, y_to = (d + 1 - 2 * k, c), (d + 2 - 4 * x, c), (d + 4 - 8 * y, c)
    z_all = (c + 1 - 2 * lax.rem(c, 2), lax.rem(c + 2, 4), 3 - c)
    owns, alls = (own_in, own_hid), (all_in, all_hid)
    piece = own_in.shape[4]
    half = piece // 2
    block = item_rows.shape[2]
    items = item_rows.shape[1]
    carried_rows = carried.shape[1]
    events = items - carried_rows

    def send(u, slot):
        w, m = UNITS[u]
        z = z_all[m]
        every = alls[w]
        if slot == 0:
            source, target, to = owns[w].at[:, y, x, k], every.at[:, c, y, x, k], (d, z)
        elif slot in (4, 6):
            spot = (
                every.at[:, z, y, 1 - x, k, 0:half] if slot == 4 else every.at[:, z, 1 - y, x, k, half : 2 * half]
            )
            source, target, to = spot, spot, (y_to if slot == 4 else x_to)
        else:
            py, px, to = {
                1: (y, x, x_to),
                2: (y, x, y_to),
                3: (y, x, core_to),
                5: (y, 1 - x, core_to),
                7: (1 - y, x, core_to),
                8: (1 - y, 1 - x, core_to),
            }[slot]
            spot = every.at[:, z, py, px, k]
            source, target = spot, spot
        return pltpu.make_async_remote_copy(
            src_ref=source,
            dst_ref=target,
            send_sem=send_sem.at[u, slot],
            recv_sem=recv_sem.at[u, slot],
            device_id=to,
            device_id_type=MESH,
        )

    def load(w):
        return pltpu.make_async_copy(owns[w], held.at[w], local_sem.at[w])

    def keep(w):
        return pltpu.make_async_copy(held.at[w], alls[w].at[:, c], local_sem.at[2 + w])

    def keep_own(_):
        for w in range(2):
            load(w).wait()
            keep(w).start()

    def item_send(m):
        return pltpu.make_async_remote_copy(
            src_ref=item_rows.at[z_all[m]],
            dst_ref=arrived.at[:, pl.ds(pl.multiple_of(c * block, block), block)],
            send_sem=row_send.at[m],
            recv_sem=row_recv.at[m],
            device_id=(d, z_all[m]),
            device_id_type=MESH,
        )

    def begin_items(_):
        for m in range(3):
            item_send(m).start()

    def item_keep():
        return pltpu.make_async_copy(
            item_rows.at[c], arrived.at[:, pl.ds(pl.multiple_of(c * block, block), block)], local_sem.at[4]
        )

    def id_copy(m):
        to = lax.rem(d + 1 + m, 8)
        return pltpu.make_async_remote_copy(
            src_ref=own_ids,
            dst_ref=all_ids.at[d],
            send_sem=id_send.at[m],
            recv_sem=id_recv.at[m],
            device_id=(to, c),
            device_id_type=MESH,
        )

    def id_keep():
        return pltpu.make_async_copy(own_ids, all_ids.at[d], local_sem.at[5])

    def begin():
        greet([(lax.rem(d + 1 + m, 8), c) for m in range(7)] + [(d, z) for z in z_all])
        id_keep().start()
        for m in range(7):
            id_copy(m).start()
        begin_z(0)
        begin_z(1)
        load(0).start()
        load(1).start()

    def begin_z(u):
        send(u, 0).start()

    def spread(u):
        send(u, 0).wait_recv()
        for slot in (1, 2, 3):
            send(u, slot).start()

    def forward(u):
        send(u, 1).wait_recv()
        send(u, 4).start()
        send(u, 5).start()
        send(u, 2).wait_recv()
        send(u, 6).start()
        send(u, 7).start()

    def far(u):
        send(u, 4).wait_recv()
        send(u, 6).wait_recv()
        send(u, 8).start()

    def close(u):
        for slot in (3, 5, 7, 8):
            send(u, slot).wait_recv()
        for slot in range(9):
            send(u, slot).wait_send()

    timeline = [(-1, begin, None), (4, keep_own, 0), (64, begin_items, 0)]
    timeline += [(at, begin_z, 2 + j) for j, at in enumerate((10, 18, 34, 50))]
    for u, at in enumerate((11, 23, 34, 46, 58, 90)):
        timeline += [(at, spread, u), (at + 12, forward, u), (at + 20, far, u)]
    timeline.sort(key=lambda entry: entry[0])
    last = 2 * n - 1

    @pl.when(i == 0)
    def _():
        padded[...] = jnp.zeros_like(padded)

    for at, action, u in timeline:
        if at < last:

            @pl.when(i == max(at, 0))
            def _(action=action, u=u):
                action() if u is None else action(u)

    @pl.when(i < n)
    def _():
        padded[0:width, :] = embed[...]

    @pl.when(i >= n)
    def _():
        padded[0:width, :] = table[...]
        padded[width : width + 1, :] = bias[...]

    spot = lax.rem(i, n) * chunk
    turned[pl.ds(pl.multiple_of(spot, chunk), chunk), :] = padded[...].T

    @pl.when(i == n - 1)
    def _():
        for z in range(4):

            def body(b, carry, z=z):
                for j in range(8):
                    row = item_ids[z * events + b * 8 + j]
                    item_rows[z, pl.ds(b * 8 + j, 1), :] = turned[pl.ds(row, 1), :]
                return carry

            lax.fori_loop(0, events // 8, body, 0)
            item_rows[z, events:items, :] = carried[z]
        item_keep().start()

    @pl.when(i == last)
    def _():
        def body(b, carry):
            for j in range(8):
                row = out_ids[b * 8 + j]
                out_rows[pl.ds(b * 8 + j, 1), :] = turned[pl.ds(row, 1), :]
            return carry

        lax.fori_loop(0, out_rows.shape[0] // 8, body, 0)
        for at, action, u in timeline:
            if at >= last:
                action(u)
        for u in range(6):
            close(u)
        for m in range(3):
            item_send(m).wait()
        for m in range(7):
            id_copy(m).wait()
        id_keep().wait()
        for w in range(2):
            keep(w).wait()
        item_keep().wait()


def gather_all(embed, table, bias, item_ids, out_ids, own_in, own_hid, carried, own_ids, collective_id):
    width, rows = embed.shape
    gates, block, units = own_in.shape
    piece = block // 8
    chunk = 128 * max(k for k in range(1, 9) if rows % (128 * k) == 0)
    n = rows // chunk
    items = item_ids.shape[0] // 4 + carried.shape[1]
    own_shape = (gates, 2, 2, 2, piece, units)
    all_shape = (gates, 4, 2, 2, 2, piece, units)
    smem = pl.BlockSpec(memory_space=pltpu.SMEM)
    hbm = pl.BlockSpec(memory_space=pl.ANY)
    all_in, all_hid, arrived, all_ids, out_rows = pl.pallas_call(
        functools.partial(head_kernel, chunk, width),
        out_shape=(
            jax.ShapeDtypeStruct(all_shape, f32),
            jax.ShapeDtypeStruct(all_shape, f32),
            jax.ShapeDtypeStruct((items, units), f32),
            jax.ShapeDtypeStruct((8,) + own_ids.shape, jnp.int32),
            jax.ShapeDtypeStruct((out_ids.shape[0], block), f32),
        ),
        grid=(2 * n,),
        in_specs=[
            smem,
            smem,
            pl.BlockSpec((width, chunk), lambda i: (0, jnp.minimum(i, n - 1))),
            pl.BlockSpec((width, chunk), lambda i: (0, jnp.maximum(i - n, 0))),
            pl.BlockSpec((1, chunk), lambda i: (0, jnp.maximum(i - n, 0))),
            hbm,
            hbm,
            pl.BlockSpec(carried.shape, lambda i: (0, 0, 0)),
            pl.BlockSpec(own_ids.shape, lambda i: (0, 0)),
        ],
        out_specs=(hbm, hbm, hbm, hbm, pl.BlockSpec((out_ids.shape[0], block), lambda i: (0, 0))),
        scratch_shapes=[
            pltpu.VMEM((block, chunk), f32),
            pltpu.VMEM((rows, block), f32),
            pltpu.VMEM((4, items, block), f32),
            pltpu.VMEM((2,) + own_shape, f32),
            pltpu.SemaphoreType.DMA((6,)),
            pltpu.SemaphoreType.DMA((6, 9)),
            pltpu.SemaphoreType.DMA((6, 9)),
            pltpu.SemaphoreType.DMA((3,)),
            pltpu.SemaphoreType.DMA((3,)),
            pltpu.SemaphoreType.DMA((7,)),
            pltpu.SemaphoreType.DMA((7,)),
        ],
        cost_estimate=takes(120),
        compiler_params=pltpu.CompilerParams(
            collective_id=collective_id, has_side_effects=True, vmem_limit_bytes=VMEM_BYTES
        ),
    )(item_ids, out_ids, embed, table, bias, own_in.reshape(own_shape), own_hid.reshape(own_shape), carried, own_ids)
    return (
        all_in.reshape(gates, 4 * block, units),
        all_hid.reshape(gates, 4 * block, units),
        arrived,
        all_ids,
        out_rows,
    )


def loss_kernel(width, factor, outs, targets, negs, loss, douts, neg_part, target_part, share, pairs, score):
    n_col, events, block = targets.shape
    n_dp, _, count, _ = negs.shape
    lane = lax.broadcasted_iota(jnp.int32, (events, block), 1)
    for c in range(n_col):
        value = jnp.where(lane < width, outs[:, c * block : (c + 1) * block], 0.0)
        value = jnp.where(lane == width, 1.0 / n_col, value)
        share[c] = value
        pairs[0, c], pairs[1, c] = split_two(value)

    @pl.loop(0, n_dp)
    def _(b):
        cols = pl.ds(pl.multiple_of(b * count, count), count)
        total = jnp.zeros((events, count), f32)
        for c in range(n_col):
            total = total + three_products((pairs[0, c], pairs[1, c]), split_two(negs[b, c]), ((1,), (1,)))
        score[:, cols] = total

    step = 32

    @pl.loop(0, events // step)
    def _(i):
        rows = pl.ds(pl.multiple_of(i * step, step), step)
        pos = jnp.zeros((step, 1), f32)
        for c in range(n_col):
            pos = pos + jnp.sum(share[c, rows, :] * targets[c, rows, :], axis=-1, keepdims=True)
        neg = score[rows, :]
        expd = jnp.exp(neg - jnp.max(neg, axis=-1, keepdims=True))
        weight = expd * (1.0 / jnp.sum(expd, axis=-1, keepdims=True))
        sig = jax.nn.sigmoid(pos - neg)
        slope = weight * sig
        ppos = jnp.sum(slope, axis=-1, keepdims=True)
        quad = jnp.sum(weight * neg * neg, axis=-1, keepdims=True)
        slope = jnp.sum(slope * (1.0 - sig), axis=-1, keepdims=True)
        loss[rows, :] = jnp.broadcast_to(quad - jnp.log(ppos), (step, LANES))
        score[rows, :] = factor * weight * (1.0 - sig * sig * (1.0 / ppos) + neg * neg + 2.0 * neg - quad)
        dpos = -factor * slope / ppos
        for c in range(n_col):
            target_part[c, rows, :] = dpos * share[c, rows, :]
            douts[rows, c * block : (c + 1) * block] = dpos * targets[c, rows, :]

    @pl.loop(0, n_dp)
    def _(b):
        dneg = score[:, pl.ds(pl.multiple_of(b * count, count), count)]
        across, down = split_two(dneg), split_two(dneg.T)
        for c in range(n_col):
            cols = slice(c * block, (c + 1) * block)
            douts[:, cols] = douts[:, cols] + three_products(across, split_two(negs[b, c]), ((1,), (0,)))
            neg_part[c, b] = three_products(down, (pairs[0, c], pairs[1, c]), ((1,), (0,)))

    for c in range(n_col):
        cols = slice(c * block, (c + 1) * block)
        douts[:, cols] = jnp.where(lane < width, douts[:, cols], 0.0)


def run_loss(outs, targets, negs, width, factor):
    n_col, events, block = targets.shape
    n_dp, _, count, _ = negs.shape
    return pl.pallas_call(
        functools.partial(loss_kernel, width, factor),
        out_shape=(
            jax.ShapeDtypeStruct((events, LANES), f32),
            jax.ShapeDtypeStruct(outs.shape, f32),
            jax.ShapeDtypeStruct((n_col, n_dp, count, block), f32),
            jax.ShapeDtypeStruct((n_col, events, block), f32),
        ),
        in_specs=[in_vmem()] * 3,
        out_specs=(in_vmem(),) * 4,
        scratch_shapes=[
            pltpu.VMEM((n_col, events, block), f32),
            pltpu.VMEM((2, n_col, events, block), bf16),
            pltpu.VMEM((events, n_dp * count), f32),
        ],
        cost_estimate=takes(25),
        compiler_params=params(),
    )(outs, targets, negs)


def back_kernel(
    steps,
    hidden,
    douts,
    keep,
    prevs,
    resets,
    updates,
    cands,
    inners,
    neg_part,
    target_part,
    own_loss,
    dgates,
    dstart,
    neg_all,
    target_all,
    loss_all,
    mine,
    core_in,
    x_in,
    y_in,
    xy_in,
    yx_in,
    z_in,
    total,
    w_high,
    w_low,
    w_flow,
    z_rows,
    flow_sem,
    load_sem,
    loss_send,
    loss_recv,
    sum_local,
    sum_send,
    sum_recv,
    row_local,
    row_send,
    row_recv,
):
    spot = Spot()
    spot.greet_all()
    rows_per, units = dstart.shape
    jobs, piece = mine.shape[0], mine.shape[4]
    step_rows = w_flow.shape[1]
    chunks = hidden.shape[0] // step_rows
    sums = SumFlow(
        spot, mine, core_in, x_in, y_in, xy_in, yx_in, z_in, total,
        lambda j, d: neg_all.at[d, pl.ds(j * piece, piece)], sum_local, sum_send, sum_recv,
    )
    rows = RowsFlow(spot, target_part, z_rows, target_all, row_local, row_send, row_recv)

    def load(i, slot):
        part = pl.ds(pl.multiple_of(i * step_rows, step_rows), step_rows)
        return pltpu.make_async_copy(hidden.at[part], w_flow.at[slot], flow_sem.at[slot])

    load(0, 0).start()
    own = []
    for j in range(jobs):
        part = pl.ds(j * piece, piece)
        own.append(pltpu.make_async_copy(neg_part.at[:, :, :, spot.k, part], mine.at[j], load_sem.at[j]))
        own[j].start()
        sums.over_core(j, neg_part.at[:, :, :, 1 - spot.k, part])
    rows.begin()
    losses = [pltpu.make_async_copy(own_loss, loss_all.at[spot.c], load_sem.at[jobs])]
    losses[0].start()
    for m, z in enumerate(spot.z_to):
        losses.append(remote(own_loss, loss_all.at[spot.c], loss_send.at[m], loss_recv.at[m], (spot.d, z)))

    @pl.loop(0, chunks)
    def _(i):
        slot = lax.rem(i, 2)

        @pl.when(i + 1 < chunks)
        def _():
            load(i + 1, 1 - slot).start()

        load(i, slot).wait()
        part = pl.ds(pl.multiple_of(i * step_rows, step_rows), step_rows)
        w_high[part, :], w_low[part, :] = split_two(w_flow[slot])

    def step(i, dstate):
        t = steps - 1 - i
        now = pl.ds(pl.multiple_of(t * rows_per, rows_per), rows_per)
        reset, update, cand = resets[now, :], updates[now, :], cands[now, :]
        dh = douts[now, :] + dstate
        dcand = dh * (1.0 - update) * (1.0 - cand * cand)
        dreset = dcand * inners[now, :] * reset * (1.0 - reset)
        dupdate = dh * (prevs[now, :] - cand) * update * (1.0 - update)
        dinner = dcand * reset
        dgates[now, 0:units] = dreset
        dgates[now, units : 2 * units] = dupdate
        dgates[now, 2 * units : 3 * units] = dinner
        dgates[now, 3 * units : 4 * units] = dcand
        total_now = dh * update
        for g, part in enumerate((dreset, dupdate, dinner)):
            pair = two_part(part)
            sect = slice(g * units, (g + 1) * units)
            first = jnp.dot(pair, w_high[sect, :], preferred_element_type=f32)
            second = jnp.dot(pair, w_low[sect, :], preferred_element_type=f32)
            total_now = total_now + (first[:rows_per] + first[rows_per:] + second[:rows_per])
        return keep[now, :] * total_now

    def sums_core(j):
        own[j].wait()
        sums.core(j)

    A, B, C, Z, S = sums_core, sums.first, sums.second, sums.along, sums.share
    timeline = (
        (0.0, ((A, 0), (A, 1))),
        (0.15, ((rows.forward, 0),)),
        (0.28, ((rows.spread, 1), (B, 0))),
        (0.38, ((rows.forward, 1), (rows.far, 0))),
        (0.47, ((B, 1), (rows.spread, 2))),
        (0.56, ((C, 0), (rows.forward, 2), (rows.far, 1))),
        (0.66, ((C, 1), (rows.spread, 3))),
        (0.78, ((Z, 0), (rows.forward, 3), (rows.far, 2))),
        (0.88, ((Z, 1), (S, 0))),
    )
    state, done = jnp.zeros((rows_per, units), f32), 0
    for share_done, actions in timeline:
        until = int(share_done * steps)
        if until > done:
            state, done = lax.fori_loop(done, until, step, state), until
        for action, argument in actions:
            action(argument)
    dstart[...] = lax.fori_loop(done, steps, step, state)
    rows.far(3)
    S(1)
    sums.end(0)
    rows.close()
    sums.end(1)
    for copy in losses:
        copy.wait()


def run_back(hidden, douts, keep, saved, neg_part, target_part, own_loss, rows_per, steps, collective_id):
    events, units = douts.shape
    count, block = neg_part.shape[2:]
    jobs = 2
    piece = count // jobs
    hbm = pl.BlockSpec(memory_space=pl.ANY)
    step_rows = units // 4
    return pl.pallas_call(
        functools.partial(back_kernel, steps),
        out_shape=(
            jax.ShapeDtypeStruct((events, 4 * units), f32),
            jax.ShapeDtypeStruct((rows_per, units), f32),
            jax.ShapeDtypeStruct((8, count, block), f32),
            jax.ShapeDtypeStruct((8, 4, events, block), f32),
            jax.ShapeDtypeStruct((4,) + own_loss.shape, f32),
        ),
        in_specs=[hbm] + [in_vmem()] * 7 + [hbm, hbm, in_vmem()],
        out_specs=(in_vmem(), in_vmem(), hbm, hbm, hbm),
        scratch_shapes=sum_scratch(jobs, piece, block)
        + [
            pltpu.VMEM(hidden.shape, bf16),
            pltpu.VMEM(hidden.shape, bf16),
            pltpu.VMEM((2, step_rows, units), f32),
            pltpu.VMEM((4, events, block), f32),
            pltpu.SemaphoreType.DMA((2,)),
            pltpu.SemaphoreType.DMA((jobs + 1,)),
            pltpu.SemaphoreType.DMA((3,)),
            pltpu.SemaphoreType.DMA((3,)),
        ]
        + flow_sems(jobs),
        cost_estimate=takes(80),
        compiler_params=pltpu.CompilerParams(
            collective_id=collective_id, has_side_effects=True, vmem_limit_bytes=VMEM_BYTES
        ),
    )(hidden, douts, keep, *saved, neg_part.reshape(4, 2, 2, 2, count, block), target_part, own_loss)


def pad_kernel(weight, bias, out):
    own, full = weight.shape[1:]
    block = out.shape[1]
    n_col = out.shape[2] // block
    part = full // n_col
    out[...] = jnp.zeros_like(out)
    for c in range(n_col):
        out[0, 0:own, c * block : c * block + part] = weight[0, :, c * part : (c + 1) * part]
    out[0, 0:own, part : part + 1] = bias[0]


def pad_units(weight, bias, n_col, block):
    gates, own, full = weight.shape
    return pl.pallas_call(
        pad_kernel,
        out_shape=jax.ShapeDtypeStruct((gates, block, n_col * block), f32),
        grid=(gates,),
        in_specs=[
            pl.BlockSpec((1, own, full), lambda g: (g, 0, 0)),
            pl.BlockSpec((1, own, 1), lambda g: (g, 0, 0)),
        ],
        out_specs=pl.BlockSpec((1, block, n_col * block), lambda g: (g, 0, 0)),
        compiler_params=params(),
    )(weight, bias[:, :, None])


def gather_weight(own, n_dp):
    gates, block, units = own.shape
    flat = own.reshape(n_dp, gates * block // n_dp, units)
    piece = lax.dynamic_index_in_dim(flat, lax.axis_index("dp"), 0, keepdims=False)
    every = lax.all_gather(piece, ("col", "dp"))
    every = every.reshape(-1, gates, block, units)
    return jnp.moveaxis(every, 0, 1).reshape(gates, -1, units)


def reduce_weight(partial, n_dp, n_col):
    gates, rows, units = partial.shape
    block = rows // n_col
    parts = jnp.moveaxis(partial.reshape(gates, n_col, block, units), 1, 0)
    parts = jnp.moveaxis(parts.reshape(n_col, n_dp, gates * block // n_dp, units), 1, 0)
    mine = lax.psum_scatter(parts, "dp", scatter_dimension=0)
    mine = lax.psum_scatter(mine, "col", scatter_dimension=0)
    return lax.all_gather(mine, "dp").reshape(gates, block, units)


def swap_col(rows, n_col):
    return lax.all_to_all(rows, "col", split_axis=0, concat_axis=0, tiled=True)


def unpad_last(value, n_col, part):
    block = value.shape[-1] // n_col
    return value.reshape(value.shape[:-1] + (n_col, block))[..., :part].reshape(value.shape[:-1] + (n_col * part,))


def local(
    n_dp,
    n_col,
    item_ids,
    target_ids,
    negative_ids,
    reset_mask,
    carry_flags,
    carried_state,
    embed_table,
    input_weight,
    hidden_weight,
    gate_bias,
    hidden_bias,
    out_table,
    out_bias,
):
    sessions, steps = item_ids.shape
    own_sessions = sessions // n_col
    rows_per = round_up(own_sessions, ROWS8)
    width = embed_table.shape[0]
    table_rows = embed_table.shape[1]
    own_rows = table_rows // n_dp
    block = round_up(width + 1, LANES)
    units = n_col * block
    events = steps * rows_per
    direct = n_dp == 8 and n_col == 4 and block % 64 == 0 and own_sessions == rows_per
    factor = 1.0 / steps
    dp_at, col_at = lax.axis_index("dp"), lax.axis_index("col")

    def by_owner(value):
        value = jnp.moveaxis(value.reshape(n_col, own_sessions, steps), 1, 2)
        value = jnp.pad(value, ((0, 0), (0, 0), (0, rows_per - own_sessions)))
        return value.reshape(-1)

    item_flat, target_flat = by_owner(item_ids), by_owner(target_ids)
    own_keep = lax.dynamic_index_in_dim(
        by_owner(1 - reset_mask).reshape(n_col, events, 1), col_at, 0, keepdims=False
    ).astype(f32)
    valid = jnp.tile(jnp.arange(rows_per) < own_sessions, steps)
    lane = jnp.arange(units) % block
    first_pad = jnp.arange(units) == width

    own_in = pad_units(input_weight, gate_bias, n_col, block)
    no_bias = jnp.zeros_like(hidden_bias)
    own_hid = pad_units(hidden_weight, jnp.stack([no_bias, no_bias, hidden_bias]), n_col, block)

    carried = (carry_flags.astype(f32)[:, None] * carried_state).reshape(n_col, own_sessions, width)
    carried = jnp.pad(carried, ((0, 0), (0, rows_per - own_sessions), (0, block - width)))
    neg_count = negative_ids.shape[0]
    own_negs = lax.dynamic_slice_in_dim(negative_ids, dp_at * (neg_count // n_dp), neg_count // n_dp)
    out_ids = jnp.concatenate([target_flat, own_negs])
    if direct:
        own_ids = jnp.concatenate([item_flat, target_flat]).reshape(-1, LANES)
        all_in, all_hid, arrived, all_ids, out_rows = gather_all(
            embed_table, out_table, out_bias[None, :], item_flat, out_ids, own_in, own_hid, carried, own_ids, 1
        )
        all_ids = all_ids.reshape(n_dp, 2, -1)
    else:
        all_hid = gather_weight(own_hid, n_dp)
        all_in = gather_weight(own_in, n_dp)
        no_row = jnp.zeros((1, table_rows), f32)
        item_rows = gather_rows(embed_table, no_row, item_flat, block).reshape(n_col, events, block)
        arrived = swap_col(jnp.concatenate([item_rows, carried], axis=1), n_col)
        arrived = jnp.moveaxis(arrived, 0, 1).reshape(events + rows_per, units)
        out_rows = gather_rows(out_table, out_bias[None, :], out_ids, block)
        all_ids = lax.all_gather(jnp.stack([item_flat, target_flat]), "dp")
    all_hid, all_in = all_hid.reshape(-1, units), all_in.reshape(-1, units)
    inputs = jnp.where(first_pad, 1.0, arrived[:events])
    start = arrived[events:]
    all_items, all_targets = all_ids[:, 0].reshape(-1), all_ids[:, 1].reshape(-1)
    count = all_items.shape[0]
    keys = jnp.concatenate([all_items, all_targets + table_rows, negative_ids + 2 * table_rows])
    order = jnp.concatenate([jnp.tile(lax.iota(jnp.int32, count), 2), lax.iota(jnp.int32, neg_count)])
    scale = 1 << (max(count, neg_count) - 1).bit_length()
    if 3 * table_rows * scale < 2**31:
        packed = lax.sort(keys * scale + order)
        keys, order = packed // scale, packed % scale
    else:
        keys, order = lax.sort((keys, order), num_keys=1)
    low = (dp_at * own_rows).astype(jnp.int32)
    by_item = (order[:count], keys[:count])
    by_target = (order[count : 2 * count], keys[count : 2 * count] - table_rows)
    by_neg = (order[2 * count :], keys[2 * count :] - 2 * table_rows)

    out_targets = out_rows[: n_col * events].reshape(n_col, events, block)
    out_negs = out_rows[n_col * events :]
    if direct:
        *saved, outs, negs, targets = run_forward_travel(
            all_hid, all_in, inputs, own_keep, start, out_negs, out_targets, steps, width, 4
        )
    else:
        targets = swap_col(out_targets, n_col)
        negs = lax.all_gather(out_negs, ("dp", "col")).reshape(n_dp, n_col, -1, block)
        *saved, outs = run_forward(all_hid, all_in, inputs, own_keep, start, steps, width)
    prevs = saved[0]

    if direct:
        own_loss, douts, neg_part, target_part = run_loss(outs, targets, negs, width, factor)
        own_loss = jnp.pad(own_loss[:, 0].reshape(steps, rows_per).T, ((0, 0), (0, round_up(steps, LANES) - steps)))
        dgates, dstart, neg_all, target_all, loss_all = run_back(
            all_hid, douts, own_keep, saved, neg_part, target_part, own_loss, rows_per, steps, 3
        )
        loss = loss_all[:, :, :steps].reshape(sessions, steps)
        neg_all, target_all = neg_all.reshape(-1, block), target_all.reshape(-1, block)
    else:
        targets = jnp.moveaxis(targets, 0, 1).reshape(events, units)
        negs = jnp.moveaxis(negs, 1, 2).reshape(neg_count, units)
        shares = jnp.where(lane == width, 1.0 / n_col, jnp.where(lane < width, outs, 0.0))
        pos_score = jnp.sum(shares * targets, axis=-1, keepdims=True)
        neg_score = lax.dot_general(shares, negs, (((1,), (1,)), ((), ())), precision=high)
        top = jnp.max(neg_score, axis=-1, keepdims=True)
        expd = jnp.exp(neg_score - top)
        weight = expd / jnp.sum(expd, axis=-1, keepdims=True)
        sig = jax.nn.sigmoid(pos_score - neg_score)
        ppos = jnp.sum(weight * sig, axis=-1, keepdims=True)
        quad = jnp.sum(weight * neg_score * neg_score, axis=-1, keepdims=True)
        slope = jnp.sum(weight * sig * (1.0 - sig), axis=-1, keepdims=True)
        own_loss = -jnp.log(ppos) + quad
        dneg = factor * weight * (1.0 - sig * sig / ppos + neg_score * neg_score + 2.0 * neg_score - quad)
        dneg = jnp.where(valid[:, None], dneg, 0.0)
        dpos = jnp.where(valid[:, None], -factor * slope / ppos, 0.0)
        douts = jnp.dot(dneg, negs, precision=high) + dpos * targets
        douts = jnp.where(lane < width, douts, 0.0)
        neg_part = lax.dot_general(dneg, shares, (((0,), (0,)), ((), ())), precision=high)
        target_part = dpos * shares

        neg_own = lax.psum_scatter(neg_part.reshape(n_dp, -1, units), "dp", scatter_dimension=0)
        neg_own = jnp.moveaxis(neg_own.reshape(-1, n_col, block), 1, 0)
        neg_own = lax.psum_scatter(neg_own, "col", scatter_dimension=0)
        neg_all = lax.all_gather(neg_own, "dp", tiled=True)
        target_own = swap_col(jnp.moveaxis(target_part.reshape(events, n_col, block), 1, 0), n_col)
        target_all = lax.all_gather(target_own.reshape(-1, block), "dp", tiled=True)
        dgates, dstart = run_backward(all_hid, douts, own_keep, saved, rows_per, steps)
        own_loss = own_loss.reshape(steps, rows_per)[:, :own_sessions]
        loss = lax.all_gather(own_loss.T, "col", tiled=True)
    grad_out, grad_obias = scatter_rows(
        [by_target + (target_all,), by_neg + (neg_all,)],
        low,
        own_rows,
        width,
        block,
    )
    grad_obias = grad_obias[0] * n_col

    gates = input_weight.shape[0]
    if direct:
        reduced, item_all, start_all = run_tail(inputs, prevs, dgates, dstart, all_in, 2)
        grad_in, grad_hid = reduced[0], reduced[1]
        item_all = item_all.reshape(-1, block)
    else:
        dx = jnp.concatenate([dgates[:, : 2 * units], dgates[:, 3 * units :]], axis=1)
        dh = dgates[:, : 3 * units]
        hid_part = lax.dot_general(dh, prevs, (((0,), (0,)), ((), ())), precision=high)
        in_part = lax.dot_general(dx, inputs, (((0,), (0,)), ((), ())), precision=high)
        dinputs = jnp.dot(dx, all_in, precision=high)
        back = jnp.concatenate([dinputs, dstart], axis=0).reshape(events + rows_per, n_col, block)
        back = swap_col(jnp.moveaxis(back, 1, 0), n_col)
        item_all = lax.all_gather(back[:, :events].reshape(-1, block), "dp", tiled=True)
        start_all = back[:, events:]
        grad_in = reduce_weight(in_part.reshape(gates, units, units), n_dp, n_col)
        grad_hid = reduce_weight(hid_part.reshape(gates, units, units), n_dp, n_col)
    grad_carried = start_all[:, :own_sessions, :width].reshape(sessions, width)
    grad_carried = carry_flags.astype(f32)[:, None] * grad_carried
    grad_embed, _ = scatter_rows([by_item + (item_all,)], low, own_rows, width, block)
    grad_in, grad_hid = grad_in[:, :width], grad_hid[:, :width]
    return (
        loss,
        grad_embed,
        unpad_last(grad_in, n_col, width),
        unpad_last(grad_hid, n_col, width),
        grad_in[:, :, width],
        grad_hid[gates - 1, :, width],
        grad_out,
        grad_obias,
        grad_carried,
    )


def solution(mesh):
    in_specs = (
        P("dp", None),
        P("dp", None),
        P(),
        P("dp", None),
        P("dp"),
        P("dp", "col"),
        P("col", None),
        P(None, "col", None),
        P(None, "col", None),
        P(None, "col"),
        P("col"),
        P("col", None),
        P(),
    )
    out_specs = (
        P("dp", None),
        P("col", "dp"),
        P(None, "col", None),
        P(None, "col", None),
        P(None, "col"),
        P("col"),
        P("col", "dp"),
        P("dp"),
        P("dp", "col"),
    )
    body = functools.partial(local, mesh.shape["dp"], mesh.shape["col"])
    return jax.shard_map(body, mesh=mesh, in_specs=in_specs, out_specs=out_specs, check_vma=False)
```

profile of v0, /device:TPU:13, one launch (start us, length us, event | category | flops | bytes accessed | tf_op | source)
XLA Modules:
  0.0 646.2 jit_solution(811029353249292320)
XLA Ops:
  4.4 3.5 copy.43.weight
  8.9 5.2 shard_map.196
  14.0 2.4 copy.45.weight
  17.3 5.0 shard_map.197
  24.4 113.6 %shard_map.198 = (f32[3,4,2,2,2,32,1024]{6,5,4,3,2,1,0:T(8,128)}, f32[3,4,2,2,2,32,1024]{6,5,4,3,2,1,0:T(8,128)}, f32[264,1024]{1,0:T(8,128)}, s32[8,16,128]{2,1,0:T(8,128)}, f32[1280,256]{1,0:T(8,128)}) custom-call(s32[1024]{0:T(1024)} %reshape.107.item_ids, s32[1280]{0:T(1024)} %pad_add_fusion.out_ids, f32[250,37888]{1,0:T(8,128)} %embed.1, ...), custom_call_target="tpu_custom_call" | custom-call | flops 131999997952 | bytes 1048576 | tf_op jit(solution)/shard_map/pallas_call | solution.py:1034
  138.0 2.4 slice_select_fusion.inputs
  141.4 1.4 slice.74.start
  142.8 1.7 slice.75.neg_own
  145.5 84.8 %shard_map.199 = (f32[256,1024]{1,0:T(8,128)}, f32[256,1024]{1,0:T(8,128)}, f32[256,1024]{1,0:T(8,128)}, f32[256,1024]{1,0:T(8,128)}, f32[256,1024]{1,0:T(8,128)...) custom-call(f32[3072,1024]{1,0:T(8,128)} %bitcast.83, f32[3072,1024]{1,0:T(8,128)} %bitcast.81, ...), custom_call_target="tpu_custom_call" | custom-call | flops 82500001792 | bytes 1048576 | tf_op jit(solution)/shard_map/pallas_call | solution.py:316
  230.3 24.1 %shard_map.200 = (f32[256,128]{1,0:T(8,128)}, f32[256,1024]{1,0:T(8,128)}, f32[4,8,256,256]{3,2,1,0:T(8,128)}, f32[4,256,256]{2,1,0:T(8,128)}) custom-call(f32[256,1024]{1,0:T(8,128)} %get-tuple-element.43.outs, f32[4,256,256]{2,1,0:T(8,128)} %get-tuple-element.44.targets, f32[8,4,256,256]{3,2,1,0:T(8,128)} %get-tuple-element.45.negs), custom_call_target="tpu_custom_call" | custom-call | flops 27499999232 | bytes 1048576 | tf_op jit(solution)/shard_map/pallas_call | solution.py:1141
  256.2 101.4 %shard_map.201 = (f32[256,4096]{1,0:T(8,128)}, f32[8,1024]{1,0:T(8,128)}, f32[8,256,256]{2,1,0:T(8,128)}, f32[8,4,256,256]{3,2,1,0:T(8,128)}, f32[4,8,128]{2,1,0:T(8,128)}) custom-call(f32[3072,1024]{1,0:T(8,128)} %bitcast.84, f32[256,1024]{1,0:T(8,128)} %get-tuple-element.46.douts, f32[256,1]{1,0:T(8,128)} %copy.48.keep, ...), custom_call_target="tpu_custom_call" | custom-call | flops 88000004096 | bytes 1048576 | tf_op jit(solution)/shard_map/pallas_call | solution.py:1305
  359.1 11.3 %sort.14 = (s32[18432]{0:T(1024)S(1)}, s32[18432]{0:T(1024)}) sort(s32[18432]{0:T(1024)S(1)} %fusion, s32[18432]{0:T(1024)S(1)} %iota.15), dimensions={0}, to_apply=%region_0.1 | sort | flops 276480 | bytes 294912 | tf_op jit(solution)/shard_map/sort | solution.py:1465
  372.4 1.9 pad_add_fusion.2.refs_0_
  374.3 194.0 %shard_map.202 = (f32[2,3,8,32,1024]{4,3,2,1,0:T(8,128)}, f32[8,4,256,256]{3,2,1,0:T(8,128)}, f32[4,8,256]{2,1,0:T(8,128)}) custom-call(f32[256,1024]{1,0:T(8,128)} %slice_select_fusion.inputs, f32[256,1024]{1,0:T(8,128)} %get-tuple-element.47.prevs, f32[256,4096]{1,0:T(8,128)} %get-tuple-element.58.dgates, f32[8,1024]{1,0:T(8,128)} %get-tuple-element.59.dstart, ...), custom_call_target="tpu_custom_call" | custom-call | flops 209000005632 | bytes 1048576 | tf_op jit(solution)/shard_map/pallas_call | solution.py:768
  568.3 22.8 %shard_map.203 = (f32[250,4736]{1,0:T(8,128)}, f32[1,4736]{1,0:T(1,128)}) custom-call(s32[3]{0:T(128)} %pad_add_fusion.2.refs_0_, s32[8192]{0:T(1024)} %get-tuple-element.85.refs_1_, s32[8192]{0:T(1024)} %get-tuple-element.80.refs_2_, f32[8192,256]{1,0:T(8,128)} %bitcast.87), custom_call_target="tpu_custom_call" | custom-call | flops 22000001024 | bytes 1048576 | tf_op jit(solution)/shard_map/pallas_call | solution.py:111
  591.0 5.4 fusion.3
  596.4 2.4 copy.51
  598.8 3.5 reshape.120
  602.3 3.6 copy.52
  605.8 3.5 reshape.122
  611.9 2.0 convert_reduce_fusion.4
  613.9 3.1 stack.45.refs_0_
  618.3 25.6 %shard_map.204 = (f32[250,4736]{1,0:T(8,128)}, f32[1,4736]{1,0:T(1,128)}) custom-call(s32[5]{0:T(128)} %stack.45.refs_0_, s32[8192]{0:T(1024)} %get-tuple-element.86.refs_1_, s32[8192]{0:T(1024)} %get-tuple-element.77.refs_2_, f32[8192,256]{1,0:T(8,128)} %bitcast.85, s32[2048]{0:T(1024)} %slice.109.refs_4_, s32[2048]{0:T(1024)} %get-tuple-element.76.refs_5_, ...), custom_call_target="tpu_custom_call" | custom-call | flops 22000001024 | bytes 1048576 | tf_op jit(solution)/shard_map/pallas_call | solution.py:111
  643.9 1.4 multiply_reduce_fusion
  (71 shorter events, 19.5 us)
Async XLA Ops:
  3.7 4.2 copy-start.9
  8.9 5.2 copy-start
  14.0 2.4 copy-start.12
  17.3 5.1 copy-start.13
  17.3 5.1 copy-start.5
  22.4 0.6 copy-start.10
  24.4 116.0 %copy-start.7 = (s32[32,32]{1,0:T(8,128)S(1)}, s32[32,32]{1,0:T(8,128)}, u32[]{:S(2)}) copy-start(s32[32,32]{1,0:T(8,128)} %param.16) | copy-start | bytes 12292
  138.0 6.5 %copy-start.1 = (f32[1280,256]{1,0:T(8,128)S(1)}, f32[1280,256]{1,0:T(8,128)}, u32[]{:S(2)}) copy-start(f32[1280,256]{1,0:T(8,128)} %get-tuple-element.42) | copy-start | bytes 3932164
  256.2 102.7 %copy-start.8 = (s32[2048]{0:T(1024)S(1)}, s32[2048]{0:T(1024)}, u32[]{:S(2)}) copy-start(s32[2048]{0:T(1024)} %param.15) | copy-start | bytes 24580
  256.2 102.7 %copy-start.4 = (s32[8,16,128]{2,1,0:T(8,128)S(1)}, s32[8,16,128]{2,1,0:T(8,128)}, u32[]{:S(2)}) copy-start(s32[8,16,128]{2,1,0:T(8,128)} %get-tuple-element.56) | copy-start | bytes 196612
  370.4 0.6 copy-start.2
  370.4 1.9 copy-start.3
  618.3 27.0 %copy-start.6 = (f32[4,8,256]{2,1,0:T(8,128)S(1)}, f32[4,8,256]{2,1,0:T(8,128)}, u32[]{:S(2)}) copy-start(f32[4,8,256]{2,1,0:T(8,128)} %get-tuple-element.67) | copy-start | bytes 98308
  618.3 27.0 %copy-start.11 = (f32[32]{0:T(128)S(1)}, f32[32]{0:T(128)}, u32[]{:S(2)}) copy-start(f32[32]{0:T(128)} %copy-done.10) | copy-start | bytes 388
where the time goes:
time: 653 us; the launch traced here: 646 us
  Pallas kernels  576 us (88%)
  local copies, waits for them, and re-layouts  46.3 us (7%)
  other arithmetic  22.4 us (3%)
    pallas_call x1, Pallas kernels, run_tail(): pl.pallas_call(tail_kernel, out_shape=(jax.ShapeDtypeStruct((2, gates, 8,...  194 us
    pallas_call x1, Pallas kernels, gather_all(): pl.pallas_call(functools.partial(head_kernel, chunk, width), out_shape=(j...  114 us
    pallas_call x1, Pallas kernels, run_back(): pl.pallas_call(functools.partial(back_kernel, steps), out_shape=(jax.Shap...  101 us
    pallas_call x1, Pallas kernels, run_forward_travel(): pl.pallas_call(functools.partial(forward_travel_kernel, steps, width), ou...  84.8 us
    pallas_call x2, Pallas kernels, scatter_rows(): pl.pallas_call(functools.partial(scatter_kernel, width, len(lists)), out_...  48.4 us
    pallas_call x1, Pallas kernels, run_loss(): pl.pallas_call(functools.partial(loss_kernel, width, factor), out_shape=(...  24.1 us

commit v1 on v0

--- a/solution.py
+++ b/solution.py
@@ -120,6 +120,161 @@
         cost_estimate=takes(20),
         compiler_params=params(),
     )(jnp.stack(ends), *operands)
+
+
+def finish_kernel(
+    shift,
+    table_rows,
+    width,
+    low,
+    packed,
+    items,
+    targets,
+    negs,
+    grads,
+    grad_embed,
+    grad_out,
+    grad_bias,
+    grad_in,
+    grad_hid,
+    even,
+    odd,
+    item_buf,
+    target_buf,
+    neg_buf,
+    grad_buf,
+    embed_out,
+    out_out,
+    bias_out,
+    weight_out,
+    sem,
+):
+    own_rows = even.shape[0]
+    events, neg_count = item_buf.shape[0], neg_buf.shape[0]
+    n_col = grad_buf.shape[3] // even.shape[1]
+    block = even.shape[1]
+    loads = [
+        pltpu.make_async_copy(source, target, sem.at[n])
+        for n, (source, target) in enumerate(
+            ((targets, target_buf), (negs, neg_buf), (grads, grad_buf), (items, item_buf))
+        )
+    ]
+    for load in loads:
+        load.start()
+    stores = [
+        pltpu.make_async_copy(source, target, sem.at[4 + n])
+        for n, (source, target) in enumerate(
+            (
+                (out_out, grad_out),
+                (bias_out, grad_bias),
+                (weight_out.at[0], grad_in),
+                (weight_out.at[1], grad_hid),
+                (embed_out, grad_embed),
+            )
+        )
+    ]
+
+    def first_from(begin, count, bound):
+        def halve(_, ends):
+            left, right = ends
+            middle = jnp.minimum((left + right) // 2, begin + count - 1)
+            less = (left < right) & (packed[middle] < bound)
+            return jnp.where(less, middle + 1, left), jnp.where(less | (left >= right), right, middle)
+
+        return lax.fori_loop(0, count.bit_length() + 1, halve, (begin, begin + count))[0]
+
+    def add(begin, count, which, data):
+        base = low[0] + which * table_rows
+        left = first_from(begin, count, base << shift)
+        right = first_from(begin, count, (base + own_rows) << shift)
+
+        def one(i, acc):
+            key = packed[i]
+            spot, row = (key >> shift) - base, key & ((1 << shift) - 1)
+            acc[pl.ds(spot, 1), :] = acc[pl.ds(spot, 1), :] + data[pl.ds(row, 1), :]
+
+        def four(i, carry):
+            for n in range(4):
+                one(left + 4 * i + n, (even, odd)[n % 2])
+            return carry
+
+        fours = (right - left) // 4
+        lax.fori_loop(0, fours, four, 0)
+
+        def rest(i, carry):
+            one(i, even)
+            return carry
+
+        lax.fori_loop(left + 4 * fours, right, rest, 0)
+
+    def clear():
+        @pl.loop(0, own_rows // LANES)
+        def _(j):
+            rows = pl.ds(pl.multiple_of(j * LANES, LANES), LANES)
+            even[rows, :] = jnp.zeros((LANES, block), f32)
+            odd[rows, :] = jnp.zeros((LANES, block), f32)
+
+    def turn(out, bias):
+        @pl.loop(0, own_rows // LANES)
+        def _(j):
+            rows = pl.ds(pl.multiple_of(j * LANES, LANES), LANES)
+            turned = (even[rows, :] + odd[rows, :]).T
+            out[:, rows] = turned[:width]
+            if bias is not None:
+                bias[:, rows] = turned[width : width + 1] * n_col
+
+    clear()
+    loads[0].wait()
+    add(events, events, 1, target_buf)
+    loads[1].wait()
+    add(2 * events, neg_count, 2, neg_buf)
+    turn(out_out, bias_out)
+    stores[0].start()
+    stores[1].start()
+    loads[2].wait()
+    part = weight_out.shape[3] // n_col
+    for w in range(2):
+        for g in range(weight_out.shape[1]):
+            for b in range(n_col):
+                weight_out[w, g, :, b * part : (b + 1) * part] = grad_buf[w, g, 0:width, b * block : b * block + part]
+        stores[2 + w].start()
+    clear()
+    loads[3].wait()
+    add(0, events, 0, item_buf)
+    turn(embed_out, None)
+    stores[4].start()
+    for store in stores:
+        store.wait()
+
+
+def run_finish(packed, shift, low, table_rows, own_rows, width, items, targets, negs, grads):
+    events, block = items.shape
+    _, gates, _, units = grads.shape
+    n_col = units // block
+    hbm = pl.BlockSpec(memory_space=pl.ANY)
+    weight = jax.ShapeDtypeStruct((gates, width, n_col * width), f32)
+    table = jax.ShapeDtypeStruct((width, own_rows), f32)
+    return pl.pallas_call(
+        functools.partial(finish_kernel, shift, table_rows, width),
+        out_shape=(table, table, jax.ShapeDtypeStruct((1, own_rows), f32), weight, weight),
+        in_specs=[in_smem(), in_smem()] + [hbm] * 4,
+        out_specs=(hbm,) * 5,
+        scratch_shapes=[
+            pltpu.VMEM((own_rows, block), f32),
+            pltpu.VMEM((own_rows, block), f32),
+            pltpu.VMEM(items.shape, f32),
+            pltpu.VMEM(targets.shape, f32),
+            pltpu.VMEM(negs.shape, f32),
+            pltpu.VMEM(grads.shape, f32),
+            pltpu.VMEM((width, own_rows), f32),
+            pltpu.VMEM((width, own_rows), f32),
+            pltpu.VMEM((1, own_rows), f32),
+            pltpu.VMEM((2,) + weight.shape, f32),
+            pltpu.SemaphoreType.DMA((9,)),
+        ],
+        cost_estimate=takes(40),
+        compiler_params=params(),
+    )(low.reshape(1), packed, items, targets, negs, grads)
 
 
 def split_weight(weight, high_part, low_part):
@@ -1460,16 +1615,16 @@
     count = all_items.shape[0]
     keys = jnp.concatenate([all_items, all_targets + table_rows, negative_ids + 2 * table_rows])
     order = jnp.concatenate([jnp.tile(lax.iota(jnp.int32, count), 2), lax.iota(jnp.int32, neg_count)])
-    scale = 1 << (max(count, neg_count) - 1).bit_length()
-    if 3 * table_rows * scale < 2**31:
-        packed = lax.sort(keys * scale + order)
-        keys, order = packed // scale, packed % scale
+    shift = (max(count, neg_count) - 1).bit_length()
+    direct = direct and (3 * table_rows) << shift < 2**31
+    low = (dp_at * own_rows).astype(jnp.int32)
+    if direct:
+        packed = lax.sort((keys << shift) | order)
     else:
         keys, order = lax.sort((keys, order), num_keys=1)
-    low = (dp_at * own_rows).astype(jnp.int32)
-    by_item = (order[:count], keys[:count])
-    by_target = (order[count : 2 * count], keys[count : 2 * count] - table_rows)
-    by_neg = (order[2 * count :], keys[2 * count :] - 2 * table_rows)
+        by_item = (order[:count], keys[:count])
+        by_target = (order[count : 2 * count], keys[count : 2 * count] - table_rows)
+        by_neg = (order[2 * count :], keys[2 * count :] - 2 * table_rows)
 
     out_targets = out_rows[: n_col * events].reshape(n_col, events, block)
     out_negs = out_rows[n_col * events :]
@@ -1522,20 +1677,13 @@
         dgates, dstart = run_backward(all_hid, douts, own_keep, saved, rows_per, steps)
         own_loss = own_loss.reshape(steps, rows_per)[:, :own_sessions]
         loss = lax.all_gather(own_loss.T, "col", tiled=True)
-    grad_out, grad_obias = scatter_rows(
-        [by_target + (target_all,), by_neg + (neg_all,)],
-        low,
-        own_rows,
-        width,
-        block,
-    )
-    grad_obias = grad_obias[0] * n_col
-
     gates = input_weight.shape[0]
     if direct:
-        reduced, item_all, start_all = run_tail(inputs, prevs, dgates, dstart, all_in, 2)
-        grad_in, grad_hid = reduced[0], reduced[1]
-        item_all = item_all.reshape(-1, block)
+        grads, item_all, start_all = run_tail(inputs, prevs, dgates, dstart, all_in, 2)
+        grad_embed, grad_out, grad_obias, grad_in, grad_hid = run_finish(
+            packed, shift, low, table_rows, own_rows, width, item_all.reshape(-1, block), target_all, neg_all, grads
+        )
+        grad_obias = grad_obias[0]
     else:
         dx = jnp.concatenate([dgates[:, : 2 * units], dgates[:, 3 * units :]], axis=1)
         dh = dgates[:, : 3 * units]
@@ -1548,17 +1696,26 @@
         start_all = back[:, events:]
         grad_in = reduce_weight(in_part.reshape(gates, units, units), n_dp, n_col)
         grad_hid = reduce_weight(hid_part.reshape(gates, units, units), n_dp, n_col)
+        grads = jnp.stack([grad_in, grad_hid])
+        grad_in, grad_hid = (unpad_last(g[:, :width], n_col, width) for g in (grad_in, grad_hid))
+        grad_out, grad_obias = scatter_rows(
+            [by_target + (target_all,), by_neg + (neg_all,)],
+            low,
+            own_rows,
+            width,
+            block,
+        )
+        grad_obias = grad_obias[0] * n_col
+        grad_embed, _ = scatter_rows([by_item + (item_all,)], low, own_rows, width, block)
     grad_carried = start_all[:, :own_sessions, :width].reshape(sessions, width)
     grad_carried = carry_flags.astype(f32)[:, None] * grad_carried
-    grad_embed, _ = scatter_rows([by_item + (item_all,)], low, own_rows, width, block)
-    grad_in, grad_hid = grad_in[:, :width], grad_hid[:, :width]
     return (
         loss,
         grad_embed,
-        unpad_last(grad_in, n_col, width),
-        unpad_last(grad_hid, n_col, width),
-        grad_in[:, :, width],
-        grad_hid[gates - 1, :, width],
+        grad_in,
+        grad_hid,
+        grads[0, :, :width, width],
+        grads[1, gates - 1, :width, width],
         grad_out,
         grad_obias,
         grad_carried,

time: 653 us -> 622 us (0.953)
  the two profiles are of different devices: /device:TPU:13 before, /device:TPU:12 now
where the time goes in v1:
time: 622 us; the launch traced here: 611 us
  Pallas kernels  561 us (90%)
  local copies, waits for them, and re-layouts  30.7 us (5%)
  other arithmetic  18 us (3%)
    pallas_call x1, Pallas kernels, run_tail(): pl.pallas_call(tail_kernel, out_shape=(jax.ShapeDtypeStruct((2, gates, 8,...  194 us
    pallas_call x1, Pallas kernels, gather_all(): pl.pallas_call(functools.partial(head_kernel, chunk, width), out_shape=(j...  113 us
    pallas_call x1, Pallas kernels, run_back(): pl.pallas_call(functools.partial(back_kernel, steps), out_shape=(jax.Shap...  101 us
    pallas_call x1, Pallas kernels, run_forward_travel(): pl.pallas_call(functools.partial(forward_travel_kernel, steps, width), ou...  85.1 us
    pallas_call x1, Pallas kernels, run_finish(): pl.pallas_call(functools.partial(finish_kernel, shift, table_rows, width)...  34.4 us
    pallas_call x1, Pallas kernels, run_loss(): pl.pallas_call(functools.partial(loss_kernel, width, factor), out_shape=(...  24.1 us
    unnamed x30, local copies, waits for them, and re-layouts  12.6 us

profile of v1, /device:TPU:12, one launch (start us, length us, event | category | flops | bytes accessed | tf_op | source)
XLA Modules:
  0.0 611.0 jit_solution(6887834948594556874)
XLA Ops:
  6.4 0.8 multiply_bitcast_fusion
  7.9 3.5 copy.42.weight
  11.4 0.9 copy.43.bias
  12.4 5.1 shard_map.197
  17.5 2.4 copy.40.weight
  19.9 0.9 copy.41.bias
  20.8 5.0 shard_map.196
  25.8 113.0 %shard_map.198 = (f32[3,4,2,2,2,32,1024]{6,5,4,3,2,1,0:T(8,128)}, f32[3,4,2,2,2,32,1024]{6,5,4,3,2,1,0:T(8,128)}, f32[264,1024]{1,0:T(8,128)}, s32[8,16,128]{2,1,0:T(8,128)}, f32[1280,256]{1,0:T(8,128)}) custom-call(s32[1024]{0:T(1024)} %reshape.94.item_ids, s32[1280]{0:T(1024)} %pad_add_fusion.out_ids, f32[250,37888]{1,0:T(8,128)} %embed.1, ...), custom_call_target="tpu_custom_call" | custom-call | flops 131999997952 | bytes 1048576 | tf_op jit(solution)/shard_map/pallas_call | solution.py:1189
  138.9 2.3 slice_select_fusion.inputs
  141.2 2.3 slice.36
  143.5 1.7 slice.35.neg_own
  145.1 1.4 slice.34.start
  146.7 0.8 copy.45.keep
  147.5 85.1 %shard_map.199 = (f32[256,1024]{1,0:T(8,128)}, f32[256,1024]{1,0:T(8,128)}, f32[256,1024]{1,0:T(8,128)}, f32[256,1024]{1,0:T(8,128)}, f32[256,1024]{1,0:T(8,128)...) custom-call(f32[3072,1024]{1,0:T(8,128)} %bitcast.59, f32[3072,1024]{1,0:T(8,128)} %bitcast.57, ...), custom_call_target="tpu_custom_call" | custom-call | flops 82500001792 | bytes 1048576 | tf_op jit(solution)/shard_map/pallas_call | solution.py:471
  232.6 24.1 %shard_map.200 = (f32[256,128]{1,0:T(8,128)}, f32[256,1024]{1,0:T(8,128)}, f32[4,8,256,256]{3,2,1,0:T(8,128)}, f32[4,256,256]{2,1,0:T(8,128)}) custom-call(f32[256,1024]{1,0:T(8,128)} %get-tuple-element.45.outs, f32[4,256,256]{2,1,0:T(8,128)} %get-tuple-element.46.targets, f32[8,4,256,256]{3,2,1,0:T(8,128)} %get-tuple-element.47.negs), custom_call_target="tpu_custom_call" | custom-call | flops 27499999232 | bytes 1048576 | tf_op jit(solution)/shard_map/pallas_call | solution.py:1296
  256.7 1.0 slice_reduce_fusion.2
  258.5 100.7 %shard_map.201 = (f32[256,4096]{1,0:T(8,128)}, f32[8,1024]{1,0:T(8,128)}, f32[8,256,256]{2,1,0:T(8,128)}, f32[8,4,256,256]{3,2,1,0:T(8,128)}, f32[4,8,128]{2,1,0:T(8,128)}) custom-call(f32[3072,1024]{1,0:T(8,128)} %bitcast.60, f32[256,1024]{1,0:T(8,128)} %get-tuple-element.48.douts, f32[256,1]{1,0:T(8,128)} %copy.45.keep, ...), custom_call_target="tpu_custom_call" | custom-call | flops 88000004096 | bytes 1048576 | tf_op jit(solution)/shard_map/pallas_call | solution.py:1460
  359.2 193.8 %shard_map.202 = (f32[2,3,8,32,1024]{4,3,2,1,0:T(8,128)}, f32[8,4,256,256]{3,2,1,0:T(8,128)}, f32[4,8,256]{2,1,0:T(8,128)}) custom-call(f32[256,1024]{1,0:T(8,128)} %slice_select_fusion.inputs, f32[256,1024]{1,0:T(8,128)} %get-tuple-element.49.prevs, f32[256,4096]{1,0:T(8,128)} %get-tuple-element.60.dgates, f32[8,1024]{1,0:T(8,128)} %get-tuple-element.61.dstart, ...), custom_call_target="tpu_custom_call" | custom-call | flops 209000005632 | bytes 1048576 | tf_op jit(solution)/shard_map/pallas_call | solution.py:923
  553.3 11.5 %sort.10 = (s32[18432]{0:T(1024)}, s32[18432]{0:T(1024)}) sort(s32[18432]{0:T(1024)S(1)} %fusion, s32[18432]{0:T(1024)S(1)} %iota.15), dimensions={0}, to_apply=%region_0.1 | sort | flops 276480 | bytes 294912 | tf_op jit(solution)/shard_map/sort | solution.py:1622
  564.8 34.4 %shard_map.203 = (f32[250,4736]{1,0:T(8,128)}, f32[250,4736]{1,0:T(8,128)}, f32[1,4736]{1,0:T(1,128)}, f32[3,250,1000]{2,1,0:T(8,128)}, f32[3,250,1000]{2,1,0:T(8,128)}) custom-call(s32[1]{0:T(128)} %bitcast.20.low, s32[18432]{0:T(1024)} %get-tuple-element.59.packed, f32[8192,256]{1,0:T(8,128)} %bitcast.62, f32[8192,256]{1,0:T(8,128)} %bitcast.61, ...), custom_call_target="tpu_custom_call" | custom-call | flops 44000002048 | bytes 1048576 | tf_op jit(solution)/shard_map/pallas_call | solution.py:257
  599.3 3.7 copy.48
  603.0 2.3 copy.49
  606.7 1.9 slice_reduce_fusion
  608.6 1.6 slice_reduce_fusion.1
  (55 shorter events, 9.5 us)
Async XLA Ops:
  0.6 10.8 %copy-start.11 = (f32[250]{0:T(256)S(1)}, f32[250]{0:T(256)}, u32[]{:S(2)}) copy-start(f32[250]{0:T(256)} %param.23) | copy-start | bytes 3004
  5.8 0.6 copy-start.9
  11.4 6.1 copy-start.1
  17.5 2.4 copy-start.8
  138.9 7.6 %copy-start.5 = (s32[32,32]{1,0:T(8,128)S(1)}, s32[32,32]{1,0:T(8,128)}, u32[]{:S(2)}) copy-start(s32[32,32]{1,0:T(8,128)} %param.16) | copy-start | bytes 12292
  359.2 193.9 %copy-start.2 = (s32[8,16,128]{2,1,0:T(8,128)S(1)}, s32[8,16,128]{2,1,0:T(8,128)}, u32[]{:S(2)}) copy-start(s32[8,16,128]{2,1,0:T(8,128)} %get-tuple-element.58) | copy-start | bytes 196612
  359.2 194.0 %copy-start.7 = (s32[2048]{0:T(1024)S(1)}, s32[2048]{0:T(1024)}, u32[]{:S(2)}) copy-start(s32[2048]{0:T(1024)} %param.15) | copy-start | bytes 24580
  599.3 3.7 copy-start
  602.9 2.4 copy-start.4
  602.9 3.0 copy-start.3
  602.9 3.0 copy-start.10
  603.0 7.3 %copy-start.6 = (f32[4,8,128]{2,1,0:T(8,128)S(1)}, f32[4,8,128]{2,1,0:T(8,128)}, u32[]{:S(2)}) copy-start(f32[4,8,128]{2,1,0:T(8,128)} %get-tuple-element.57) | copy-start | bytes 49156
